TPU v7x, 128 devices: a whole 4x4x4 slice. The times are simulated.
128 devices in a mesh: lat: 4 (over z), lon: 32 (over x, y, core).
Axes of the slice: x: 4, y: 4, z: 4, core: 2. Of those that a mesh axis runs over, the one named last changes fastest.
Arguments:
- obs_tiles: bfloat16 [128, 128, 4, 8, 256], P(('lat', 'lon'))
- tile_block: int32 [128, 128, 4], P(('lat', 'lon')), may hold values from 0 to 11
- tile_rows: int32 [128, 128, 4], P(('lat', 'lon')), may hold values from 0 to 256, as said below
- embed_weight: bfloat16 [6, 23], replicated, may hold values from -2.5 to 2.5
- conv1_weight: bfloat16 [9, 24, 256], replicated, may hold values from -0.4375 to 0.4375
- conv1_bias: float32 [256], replicated, may hold values from -3 to 3
- conv2_weight: bfloat16 [9, 256, 512], replicated, may hold values from -0.125 to 0.125
- conv2_bias: float32 [512], replicated, may hold values from -3 to 3
Outputs:
- coarse: bfloat16 [64, 384, 512], P('lat')
Inputs may be any that keep to these rules, and one draw needn't show every extreme that they name: `tile_rows`: for each source and destination the live slots come first: all hold 256 rows but the last live one, which holds 1 to 256; later slots hold 0. In every draw one destination block receives 4 live tiles from every source.
All inputs are finite; a program needn't handle non-finite values.
Results may differ from a plain program's by a relative error of at most 0.0052.
Values may be sent and summed in bfloat16 or wider, within the bound.
No kernel may reach another device: no remote copies, remote signals or barrier semaphores. Data moves between devices by JAX's collectives and lax.ppermute only.
A program may use at most 64 MiB of HBM per device.

v0:
```python
import jax
import jax.numpy as jnp
from jax import lax
from jax.sharding import PartitionSpec as P

BX = 64
BY = 48
SB = 16
kernel_scale = 0.5


def shifted(value, axis, by):
    length = lax.axis_size(axis)
    return lax.ppermute(value, axis, [(i, (i + by) % length) for i in range(length)])


def from_behind(block, axis, distance):
    devices = range(lax.axis_size(axis))
    route = [(i - distance, i) for i in devices if i - distance in devices]
    return lax.ppermute(block, axis, route)


def tile_terms(tiles, row_count, embed_weight):
    cell_ids = jnp.arange(SB * SB, dtype=jnp.int32)
    center_row = (cell_ids // SB).astype(jnp.float32) + 0.5
    center_col = (cell_ids % SB).astype(jnp.float32) + 0.5
    place_row = tiles[:, 0, :].astype(jnp.float32)
    place_col = tiles[:, 1, :].astype(jnp.float32)
    distance = (center_row[None, :, None] - place_row[:, None, :]) ** 2 + (
        center_col[None, :, None] - place_col[:, None, :]
    ) ** 2
    is_live = jnp.arange(tiles.shape[2], dtype=jnp.int32)[None, None, :] < row_count[:, None, None]
    kernel = jnp.where(is_live, jnp.exp(-distance * kernel_scale), jnp.float32(0.0)).astype(
        jnp.bfloat16
    )
    embedded = jnp.einsum(
        "tvo,vc->tco", tiles[:, 2:, :], embed_weight, preferred_element_type=jnp.float32
    ).astype(jnp.bfloat16)
    features = jnp.concatenate(
        [jnp.ones((tiles.shape[0], 1, tiles.shape[2]), jnp.bfloat16), embedded], axis=1
    )
    return jnp.einsum("tco,tko->tck", features, kernel, preferred_element_type=jnp.float32)


def stride_conv(padded, weight, out_rows, out_cols):
    running = jnp.zeros((out_rows * out_cols, weight.shape[2]), jnp.float32)
    for row_tap in range(3):
        for col_tap in range(3):
            tap_rows = lax.slice(
                padded,
                (row_tap, col_tap, 0),
                (row_tap + 2 * out_rows - 1, col_tap + 2 * out_cols - 1, padded.shape[2]),
                (2, 2, 1),
            )
            running = running + jnp.dot(
                tap_rows.reshape(-1, padded.shape[2]),
                weight[3 * row_tap + col_tap],
                preferred_element_type=jnp.float32,
            )
    return running.reshape(out_rows, out_cols, weight.shape[2])


def shards(
    obs_tiles,
    tile_block,
    tile_rows,
    embed_weight,
    conv1_weight,
    conv1_bias,
    conv2_weight,
    conv2_bias,
):
    block_count = obs_tiles.shape[1]
    slot_count = obs_tiles.shape[2]
    feat_rows = obs_tiles.shape[3]
    tile_len = obs_tiles.shape[4]
    arrived_all = (
        lax.all_to_all(obs_tiles, ("lat", "lon"), split_axis=1, concat_axis=0, tiled=True),
        lax.all_to_all(tile_block, ("lat", "lon"), split_axis=1, concat_axis=0, tiled=True),
        lax.all_to_all(tile_rows, ("lat", "lon"), split_axis=1, concat_axis=0, tiled=True),
    )
    group_count = block_count // 8
    group_size = 8 * slot_count
    arrived = arrived_all[0].reshape(group_count, group_size, feat_rows, tile_len)
    block_ids = arrived_all[1].reshape(group_count, group_size)
    row_count = arrived_all[2].reshape(group_count, group_size)
    sub_count = BX // SB * (BY // SB)
    channel_count = conv1_weight.shape[1]

    def add_group(running, inputs):
        tiles, group_ids, group_rows = inputs
        tile_sums = tile_terms(tiles, group_rows, embed_weight)
        onehot = (group_ids[:, None] == jnp.arange(sub_count, dtype=jnp.int32)[None, :]).astype(
            jnp.float32
        )
        return (
            running + jnp.einsum("ts,tck->sck", onehot, tile_sums, precision=lax.Precision.HIGHEST),
            None,
        )

    start = jnp.zeros((sub_count, channel_count, tile_len), jnp.float32)
    block_sums, _ = lax.scan(add_group, start, (arrived, block_ids, row_count))
    density = block_sums[:, 0, :]
    data_part = block_sums[:, 1:, :] / (1.0 + density[:, None, :])
    channels = jnp.concatenate([jnp.log1p(density)[:, None, :], data_part], axis=1).astype(
        jnp.bfloat16
    )
    grid_field = (
        channels.reshape(BX // SB, BY // SB, channel_count, SB, SB)
        .transpose(0, 3, 1, 4, 2)
        .reshape(BX, BY, channel_count)
    )
    rim_width = 1
    side_rim = shifted(grid_field[:, BY - rim_width :, :], "lon", 1)
    padded = jnp.concatenate([side_rim, grid_field], axis=1)
    top_rim = from_behind(padded[BX - rim_width :, :, :], "lat", 1)
    padded = jnp.concatenate([top_rim, padded], axis=0)
    first_layer = jax.nn.silu(
        stride_conv(padded, conv1_weight, BX // 2, BY // 2) + conv1_bias
    ).astype(jnp.bfloat16)
    first_side = shifted(first_layer[:, BY // 2 - 1 :, :], "lon", 1)
    first_padded = jnp.concatenate([first_side, first_layer], axis=1)
    first_top = from_behind(first_padded[BX // 2 - 1 :, :, :], "lat", 1)
    first_padded = jnp.concatenate([first_top, first_padded], axis=0)
    coarse = (stride_conv(first_padded, conv2_weight, BX // 4, BY // 4) + conv2_bias).astype(
        jnp.bfloat16
    )
    return lax.all_gather(coarse, "lon", axis=1, tiled=True)


def solution(mesh):
    placed = (
        P(("lat", "lon"), None, None, None, None),
        P(("lat", "lon"), None, None),
        P(("lat", "lon"), None, None),
        P(),
        P(),
        P(),
        P(),
        P(),
    )
    return jax.shard_map(
        shards, mesh=mesh, in_specs=placed, out_specs=P("lat", None, None), check_vma=False
    )
```

profile of v0, /device:TPU:1, one launch (start us, length us, event | category | flops | bytes accessed | tf_op | source)
XLA Modules:
  0.0 268.7 jit_solution(6266015869091623327)
XLA Ops:
  6.5 1.4 copy.26
  8.0 11.5 %all-to-all-start = ((s32[1,128,4]{2,0,1:T(1,128)}), s32[1,128,4]{2,0,1:T(1,128)S(1)}, u32[]{:S(2)}, u32[]{:S(2)}) async-start(s32[1,128,4]{2,0,1:T(1,128)} %copy.26), calls=%async_computation | async-start | bytes 131072 | tf_op jit(solution)/shard_map/all_to_all | solution.py:79
  20.3 8.7 %all-to-all-done = s32[1,128,4]{2,0,1:T(1,128)S(1)} async-done(((s32[1,128,4]{2,0,1:T(1,128)}), s32[1,128,4]{2,0,1:T(1,128)S(1)}, u32[]{:S(2)}, u32[]{:S(2)}) %all-to-all-start) | async-done | bytes 2080 | tf_op jit(solution)/shard_map/all_to_all | solution.py:79
  29.0 13.8 %all_to_all.12 = s32[1,128,4]{2,0,1:T(1,128)S(1)} all-to-all(s32[1,128,4]{2,0,1:T(1,128)S(1)} %copy.28), channel_id=1, replica_groups=mesh['lat'=4,'lon'=32] {'lat','lon'}, dimensions={1} | all-to-all | bytes 4096 | tf_op jit(solution)/shard_map/all_to_all | solution.py:80
  42.8 4.4 %all-to-all-start.1 = ((bf16[1,128,4,8,256]{4,3,2,0,1:T(8,128)(2,1)}), bf16[1,128,4,8,256]{4,3,2,0,1:T(8,128)(2,1)S(1)}, u32[]{:S(2)}, u32[]{:S(2)}) async-start(bf16[1,128,4,8,256]{4,3,2,0,1:T(8,128)(2,1)} %bitcast.136), calls=%async_computation.1 | async-start | bytes 4194304 | tf_op jit(solution)/shard_map/all_to_all | solution.py:78
  49.5 28.2 %all-to-all-done.1 = bf16[1,128,4,8,256]{4,3,2,0,1:T(8,128)(2,1)S(1)} async-done(((bf16[1,128,4,8,256]{4,3,2,0,1:T(8,128)(2,1)}), bf16[1,128,4,8,256]{4,3,2,0,1:T(8,128)(2,1)S(1)}, u32[]{:S(2)}, u32[]{:S(2)}) %all-to-all-start.1) | async-done | bytes 2097184 | tf_op jit(solution)/shard_map/all_to_all | solution.py:78
  77.7 61.0 %while.13 = (s32[]{:T(128)}, f32[12,24,256]{2,0,1:T(8,128)S(1)}, s32[16,32]{1,0:T(8,128)S(1)}, bf16[16,32,8,256]{3,2,1,0:T(8,128)(2,1)S(1)}, bf16[6,23]{1,0:T(8,...) while((s32[]{:T(128)}, f32[12,24,256]{2,0,1:T(8,128)S(1)}, ...), condition=%wide.region_1.2_spmd.clone, body=%wide.region_0.1_spmd.clone.sunk | while | flops 150475136 | bytes 3626115 | solution.py:102
  78.2 2.7 fusion.104
  82.0 2.7 fusion.104
  85.8 2.7 fusion.104
  89.6 2.7 fusion.104
  93.5 2.7 fusion.104
  97.3 2.7 fusion.104
  101.1 2.7 fusion.104
  104.9 2.7 fusion.104
  108.7 2.7 fusion.104
  112.5 2.7 fusion.104
  116.3 2.7 fusion.104
  120.2 2.7 fusion.104
  124.0 2.7 fusion.104
  127.8 2.7 fusion.104
  131.6 2.7 fusion.104
  135.4 2.7 fusion.104
  140.0 1.1 copy.30
  141.8 1.6 slice.164
  143.4 1.7 slice.162
  147.6 0.9 fusion.53
  148.6 1.8 fusion.51
  150.4 0.9 fusion.48
  151.3 0.9 fusion.46
  153.8 0.9 fusion.25
  154.7 2.0 collective-permute-start.1
  156.7 3.7 %slice.160 = bf16[32,24,24]{0,2,1:T(8,128)(2,1)S(1)} slice(bf16[64,49,24]{0,2,1:T(8,128)(2,1)S(1)} %pad_maximum_fusion.1), slice={[1:64:2], [0:47:2], [0:24:1]} | slice | bytes 73728 | tf_op jit(solution)/shard_map/slice | solution.py:49
  160.4 3.7 %slice.154 = bf16[32,24,24]{0,2,1:T(8,128)(2,1)S(1)} slice(bf16[64,49,24]{0,2,1:T(8,128)(2,1)S(1)} %pad_maximum_fusion.1), slice={[0:63:2], [0:47:2], [0:24:1]} | slice | bytes 73728 | tf_op jit(solution)/shard_map/slice | solution.py:49
  166.2 1.1 maximum_maximum_fusion.1
  167.3 4.2 %slice.152 = bf16[32,24,24]{0,2,1:T(8,128)(2,1)S(1)} slice(bf16[65,49,24]{0,2,1:T(8,128)(2,1)S(1)} %maximum_maximum_fusion.1), slice={[0:63:2], [2:49:2], [0:24:1]} | slice | bytes 73728 | tf_op jit(solution)/shard_map/slice | solution.py:49
  171.5 3.7 %slice.150 = bf16[32,24,24]{0,2,1:T(8,128)(2,1)S(1)} slice(bf16[65,49,24]{0,2,1:T(8,128)(2,1)S(1)} %maximum_maximum_fusion.1), slice={[0:63:2], [1:48:2], [0:24:1]} | slice | bytes 73728 | tf_op jit(solution)/shard_map/slice | solution.py:49
  175.2 3.7 %slice.148 = bf16[32,24,24]{0,2,1:T(8,128)(2,1)S(1)} slice(bf16[65,49,24]{0,2,1:T(8,128)(2,1)S(1)} %maximum_maximum_fusion.1), slice={[0:63:2], [0:47:2], [0:24:1]} | slice | bytes 73728 | tf_op jit(solution)/shard_map/slice | solution.py:49
  179.4 0.9 reshape.151
  180.8 1.1 fusion.58
  181.8 1.0 convolution_add_fusion.4
  182.8 1.0 convolution_add_fusion.3
  183.9 1.0 fusion.23
  184.9 1.0 fusion.24
  191.9 2.1 collective-permute-start.3
  196.0 1.0 maximum_maximum_fusion
  201.4 51.4 %all-gather.2.cloned.1.call-done = bf16[16,384,512]{2,0,1:T(8,128)(2,1)} async-done(((bf16[16,12,512]{2,0,1:T(8,128)(2,1)}), bf16[16,384,512]{2,0,1:T(8,128)(2,1)}) %all-gather.2.cloned.1.call-update) | async-done | bytes 6291472 | tf_op jit(solution)/shard_map/all_gather | solution.py:128
  252.8 9.0 %copy.39 = bf16[16,384,512]{2,1,0:T(8,128)(2,1)} copy(bf16[16,384,512]{2,0,1:T(8,128)(2,1)} %all-gather.2.cloned.1.call-done) | data formatting | bytes 12582912 | tf_op jit(solution)/shard_map/all_gather | solution.py:128
  (224 shorter events, 41.6 us)
Async XLA Ops:
  8.0 21.0 %all-to-all-start = ((s32[1,128,4]{2,0,1:T(1,128)}), s32[1,128,4]{2,0,1:T(1,128)S(1)}, u32[]{:S(2)}, u32[]{:S(2)}) async-start(s32[1,128,4]{2,0,1:T(1,128)} %copy.26), calls=%async_computation | async-start | bytes 131072 | tf_op jit(solution)/shard_map/all_to_all | solution.py:79
  20.2 57.5 %copy-start.10 = (bf16[6,23]{1,0:T(8,128)(2,1)S(1)}, bf16[6,23]{1,0:T(8,128)(2,1)}, u32[]{:S(2)}) copy-start(bf16[6,23]{1,0:T(8,128)(2,1)} %param.13) | copy-start | bytes 832
  42.8 34.9 %all-to-all-start.1 = ((bf16[1,128,4,8,256]{4,3,2,0,1:T(8,128)(2,1)}), bf16[1,128,4,8,256]{4,3,2,0,1:T(8,128)(2,1)S(1)}, u32[]{:S(2)}, u32[]{:S(2)}) async-start(bf16[1,128,4,8,256]{4,3,2,0,1:T(8,128)(2,1)} %bitcast.136), calls=%async_computation.1 | async-start | bytes 4194304 | tf_op jit(solution)/shard_map/all_to_all | solution.py:78
  47.2 205.6 %all-gather.2.cloned.1.call-start = ((), (), s32[]{:S(2)}) async-start(), calls=%async_computation.3 | async-start | bytes 6488064 | tf_op jit(solution)/shard_map/all_gather | solution.py:128
  146.8 6.2 %collective-permute-start = (bf16[64,1,24]{2,1,0:T(2,128)(2,1)}, bf16[64,1,24]{2,1,0:T(2,128)(2,1)}, u32[]{:S(2)}, u32[]{:S(2)}) collective-permute-start(bf16[64,1,24]{2,1,0:T(2,128)(2,1)} %slice.192), channel_id=1, source_target_pairs={{0,1},{1,2},{2,3},{3,4},{4,5},{5,6},{6,7},{7,8},{8,9},{9,10},{10,1... | collective-permute-start | bytes 9224 | tf_op jit(solution)/shard_map/ppermute | solution.py:14
  154.7 11.5 %collective-permute-start.1 = (bf16[1,49,24]{0,2,1:T(8,128)(2,1)}, bf16[1,49,24]{0,2,1:T(8,128)(2,1)}, u32[]{:S(2)}, u32[]{:S(2)}) collective-permute-start(bf16[1,49,24]{0,2,1:T(8,128)(2,1)} %fusion.25), channel_id=1, source_target_pairs={{0,32},{32,64},{64,96},{1,33},{33,65},{65,97},{2,34},{34,66},{66,9... | collective-permute-start | bytes 7064 | tf_op jit(solution)/shard_map/ppermute | solution.py:20
  180.3 3.5 %copy-start = (f32[768,256]{1,0:T(8,128)S(1)}, f32[768,256]{1,0:T(8,128)}, u32[]{:S(2)}) copy-start(f32[768,256]{1,0:T(8,128)} %fusion.51) | copy-start | bytes 2359300
  180.5 3.4 %copy-start.9 = (bf16[768,24]{0,1:T(8,128)(2,1)S(1)}, bf16[768,24]{0,1:T(8,128)(2,1)}, u32[]{:S(2)}) copy-start(bf16[768,24]{0,1:T(8,128)(2,1)} %reshape.154) | copy-start | bytes 110596
  182.8 2.1 copy-start.8
  184.9 1.0 copy-start.12
  186.2 5.1 %collective-permute-start.2 = (bf16[32,1,256]{2,1,0:T(2,128)(2,1)S(1)}, bf16[32,1,256]{2,1,0:T(2,128)(2,1)S(1)}, u32[]{:S(2)}, u32[]{:S(2)}) collective-permute-start(bf16[32,1,256]{2,1,0:T(2,128)(2,1)S(1)} %slice.195), channel_id=1, source_target_pairs={{0,1},{1,2},{2,3},{3,4},{4,5},{5,6},{6,7},{7,8},{8,9},{9,10},{10,1... | collective-permute-start | bytes 49160 | tf_op jit(solution)/shard_map/ppermute | solution.py:14
  191.3 7.1 %copy-start.1 = (bf16[9,256,512]{2,1,0:T(8,128)(2,1)S(1)}, bf16[9,256,512]{2,1,0:T(8,128)(2,1)}, u32[]{:S(2)}) copy-start(bf16[9,256,512]{2,1,0:T(8,128)(2,1)} %param.16) | copy-start | bytes 7077892
  191.3 2.7 copy-start.7
  191.9 4.1 %collective-permute-start.3 = (bf16[1,25,256]{2,1,0:T(8,128)(2,1)}, bf16[1,25,256]{2,1,0:T(8,128)(2,1)S(1)}, u32[]{:S(2)}, u32[]{:S(2)}) collective-permute-start(bf16[1,25,256]{2,1,0:T(8,128)(2,1)} %fusion.45), channel_id=1, source_target_pairs={{0,32},{32,64},{64,96},{1,33},{33,65},{65,97},{2,34},{34,66},{66,9... | collective-permute-start | bytes 38408 | tf_op jit(solution)/shard_map/ppermute | solution.py:20
  197.0 2.0 copy-start.6
  198.3 1.0 copy-start.5
  198.6 0.9 copy-start.4
  199.1 0.9 copy-start.3
  199.3 0.9 copy-start.2
  199.7 0.7 copy-start.11
Sparse Core Ops, SparseCore 0:
  201.5 51.2 all-gather.1
where the time goes:
time: 270 us; the launch traced here: 269 us
  waiting for transfers between devices  88.4 us (33%)
  matrix products  69.2 us (26%)
  local copies, waits for them, and re-layouts  53.3 us (20%)
  starting transfers between devices  20.9 us (8%)
  between operations  14 us (5%)
  blocking collectives  13.8 us (5%)
  other arithmetic  7.95 us (3%)
    all_gather x1, waiting for transfers between devices, shards(): return lax.all_gather(coarse, 'lon', axis=1, tiled=True)  51.4 us
    dot_general x16, matrix products, tile_terms(): jnp.einsum('tco,tko->tck', features, kernel, preferred_element_type=jnp.f...  42.6 us
    slice x23, local copies, waits for them, and re-layouts, stride_conv(): lax.slice(padded, (row_tap, col_tap, 0), (row_tap + 2 * out_rows - 1, col...  29.3 us
    all_to_all x1, waiting for transfers between devices, shards(): lax.all_to_all(obs_tiles, ('lat', 'lon'), split_axis=1, concat_axis=0, ti...  28.2 us
    all_to_all x1, blocking collectives, shards(): lax.all_to_all(tile_rows, ('lat', 'lon'), split_axis=1, concat_axis=0, ti...  13.8 us
    dot_general x18, matrix products, stride_conv(): jnp.dot(tap_rows.reshape(-1, padded.shape[2]), weight[3 * row_tap + col_t...  11.6 us
    all_to_all x1, starting transfers between devices, shards(): lax.all_to_all(tile_block, ('lat', 'lon'), split_axis=1, concat_axis=0, t...  11.5 us
    dot_general x16, matrix products, add_group(): jnp.einsum('ts,tck->sck', onehot, tile_sums, precision=lax.Precision.HIGH...  10.1 us
  transfers between devices with their start and end apart: 7, of which 3 were waited for; matrix products, arithmetic and copies ran while one was open for 9% of the time, Pallas kernels for 0%

commit v1 on v0

--- a/solution.py
+++ b/solution.py
@@ -125,7 +125,9 @@
     coarse = (stride_conv(first_padded, conv2_weight, BX // 4, BY // 4) + conv2_bias).astype(
         jnp.bfloat16
     )
-    return lax.all_gather(coarse, "lon", axis=1, tiled=True)
+    return jnp.concatenate(
+        lax.all_to_all(jnp.stack([coarse] * lax.axis_size("lon")), "lon", 0, 0), axis=1
+    )
 
 
 def solution(mesh):

time: 270 us -> 283 us (1.048)
  blocking collectives: 13.8 us -> 95.3 us
  waiting for transfers between devices: 88.4 us -> 37 us
  between operations: 14 us -> 0.67 us
  local copies, waits for them, and re-layouts: 53.3 us -> 49.4 us
    all_to_all x0 -> x1, blocking collectives: none -> 81.5 us  [shards(): lax.all_to_all(jnp.stack([coarse] * lax.axis_size('lon')), 'lon', 0, 0)]
    all_gather x1 -> x0, waiting for transfers between devices: 51.4 us -> none  [shards(): return lax.all_gather(coarse, 'lon', axis=1, tiled=True)]
    all_gather x1 -> x0, local copies, waits for them, and re-layouts: 9.02 us -> none  [shards(): return lax.all_gather(coarse, 'lon', axis=1, tiled=True)]
    reshape x0 -> x1, local copies, waits for them, and re-layouts: none -> 6.36 us  [shards(): jnp.concatenate(lax.all_to_all(jnp.stack([coarse] * lax.axis_size('lon'))...]
  transfers between devices with their start and end apart: 7 -> 6, of which waited for: 3 -> 2; matrix products, arithmetic and copies ran while one was open for 9% -> 9% of each run, Pallas kernels for 0% -> 0%
where the time goes in v1:
time: 283 us; the launch traced here: 281 us
  blocking collectives  95.3 us (34%)
  matrix products  69.2 us (24%)
  local copies, waits for them, and re-layouts  49.4 us (17%)
  waiting for transfers between devices  37 us (13%)
  starting transfers between devices  20.9 us (7%)
  other arithmetic  7.96 us (3%)
    all_to_all x1, blocking collectives, shards(): lax.all_to_all(jnp.stack([coarse] * lax.axis_size('lon')), 'lon', 0, 0)  81.5 us
    dot_general x16, matrix products, tile_terms(): jnp.einsum('tco,tko->tck', features, kernel, preferred_element_type=jnp.f...  42.6 us
    slice x23, local copies, waits for them, and re-layouts, stride_conv(): lax.slice(padded, (row_tap, col_tap, 0), (row_tap + 2 * out_rows - 1, col...  29.4 us
    all_to_all x1, waiting for transfers between devices, shards(): lax.all_to_all(obs_tiles, ('lat', 'lon'), split_axis=1, concat_axis=0, ti...  28.2 us
    all_to_all x1, blocking collectives, shards(): lax.all_to_all(tile_rows, ('lat', 'lon'), split_axis=1, concat_axis=0, ti...  13.8 us
    dot_general x18, matrix products, stride_conv(): jnp.dot(tap_rows.reshape(-1, padded.shape[2]), weight[3 * row_tap + col_t...  11.6 us
    all_to_all x1, starting transfers between devices, shards(): lax.all_to_all(tile_block, ('lat', 'lon'), split_axis=1, concat_axis=0, t...  11.5 us
    dot_general x16, matrix products, add_group(): jnp.einsum('ts,tck->sck', onehot, tile_sums, precision=lax.Precision.HIGH...  10.1 us
  transfers between devices with their start and end apart: 6, of which 2 were waited for; matrix products, arithmetic and copies ran while one was open for 9% of the time, Pallas kernels for 0%

profile of v1, /device:TPU:1, one launch (start us, length us, event | category | flops | bytes accessed | tf_op | source)
XLA Modules:
  0.0 281.4 jit_solution(16323616203619833429)
XLA Ops:
  0.0 1.4 copy.28
  1.4 11.5 %all-to-all-start = ((s32[1,128,4]{2,0,1:T(1,128)}), s32[1,128,4]{2,0,1:T(1,128)S(1)}, u32[]{:S(2)}, u32[]{:S(2)}) async-start(s32[1,128,4]{2,0,1:T(1,128)} %copy.28), calls=%async_computation | async-start | bytes 131072 | tf_op jit(solution)/shard_map/all_to_all | solution.py:79
  13.7 8.7 %all-to-all-done = s32[1,128,4]{2,0,1:T(1,128)S(1)} async-done(((s32[1,128,4]{2,0,1:T(1,128)}), s32[1,128,4]{2,0,1:T(1,128)S(1)}, u32[]{:S(2)}, u32[]{:S(2)}) %all-to-all-start) | async-done | bytes 2080 | tf_op jit(solution)/shard_map/all_to_all | solution.py:79
  22.5 13.8 %all_to_all.32 = s32[1,128,4]{2,0,1:T(1,128)S(1)} all-to-all(s32[1,128,4]{2,0,1:T(1,128)S(1)} %copy.30), channel_id=1, replica_groups=mesh['lat'=4,'lon'=32] {'lat','lon'}, dimensions={1} | all-to-all | bytes 4096 | tf_op jit(solution)/shard_map/all_to_all | solution.py:80
  36.3 4.4 %all-to-all-start.1 = ((bf16[1,128,4,8,256]{4,3,2,0,1:T(8,128)(2,1)}), bf16[1,128,4,8,256]{4,3,2,0,1:T(8,128)(2,1)S(1)}, u32[]{:S(2)}, u32[]{:S(2)}) async-start(bf16[1,128,4,8,256]{4,3,2,0,1:T(8,128)(2,1)} %bitcast.140), calls=%async_computation.1 | async-start | bytes 4194304 | tf_op jit(solution)/shard_map/all_to_all | solution.py:78
  42.9 28.2 %all-to-all-done.1 = bf16[1,128,4,8,256]{4,3,2,0,1:T(8,128)(2,1)S(1)} async-done(((bf16[1,128,4,8,256]{4,3,2,0,1:T(8,128)(2,1)}), bf16[1,128,4,8,256]{4,3,2,0,1:T(8,128)(2,1)S(1)}, u32[]{:S(2)}, u32[]{:S(2)}) %all-to-all-start.1) | async-done | bytes 2097184 | tf_op jit(solution)/shard_map/all_to_all | solution.py:78
  71.2 61.0 %while.13 = (s32[]{:T(128)}, f32[12,24,256]{2,0,1:T(8,128)S(1)}, s32[16,32]{1,0:T(8,128)S(1)}, bf16[16,32,8,256]{3,2,1,0:T(8,128)(2,1)S(1)}, bf16[6,23]{1,0:T(8,...) while((s32[]{:T(128)}, f32[12,24,256]{2,0,1:T(8,128)S(1)}, ...), condition=%wide.region_1.2_spmd.clone, body=%wide.region_0.1_spmd.clone.sunk | while | flops 150475136 | bytes 3626115 | solution.py:102
  71.7 2.7 fusion.104
  75.5 2.7 fusion.104
  79.3 2.7 fusion.104
  83.1 2.7 fusion.104
  86.9 2.7 fusion.104
  90.7 2.7 fusion.104
  94.6 2.7 fusion.104
  98.4 2.7 fusion.104
  102.2 2.7 fusion.104
  106.0 2.7 fusion.104
  109.8 2.7 fusion.104
  113.6 2.7 fusion.104
  117.4 2.7 fusion.104
  121.3 2.7 fusion.104
  125.1 2.7 fusion.104
  128.9 2.7 fusion.104
  133.5 1.1 copy.32
  134.6 1.7 slice.164
  136.3 1.7 slice.162
  140.5 0.9 fusion.53
  141.5 1.8 fusion.51
  143.3 0.9 fusion.48
  144.2 0.9 fusion.46
  145.9 0.9 fusion.25
  146.8 2.0 collective-permute-start.1
  148.9 3.7 %slice.160 = bf16[32,24,24]{0,2,1:T(8,128)(2,1)S(1)} slice(bf16[64,49,24]{0,2,1:T(8,128)(2,1)S(1)} %pad_maximum_fusion.1), slice={[1:64:2], [0:47:2], [0:24:1]} | slice | bytes 73728 | tf_op jit(solution)/shard_map/slice | solution.py:49
  152.6 3.7 %slice.154 = bf16[32,24,24]{0,2,1:T(8,128)(2,1)S(1)} slice(bf16[64,49,24]{0,2,1:T(8,128)(2,1)S(1)} %pad_maximum_fusion.1), slice={[0:63:2], [0:47:2], [0:24:1]} | slice | bytes 73728 | tf_op jit(solution)/shard_map/slice | solution.py:49
  156.4 0.9 reshape.163
  158.3 1.1 maximum_maximum_fusion.1
  159.5 4.2 %slice.152 = bf16[32,24,24]{0,2,1:T(8,128)(2,1)S(1)} slice(bf16[65,49,24]{0,2,1:T(8,128)(2,1)S(1)} %maximum_maximum_fusion.1), slice={[0:63:2], [2:49:2], [0:24:1]} | slice | bytes 73728 | tf_op jit(solution)/shard_map/slice | solution.py:49
  163.7 3.7 %slice.150 = bf16[32,24,24]{0,2,1:T(8,128)(2,1)S(1)} slice(bf16[65,49,24]{0,2,1:T(8,128)(2,1)S(1)} %maximum_maximum_fusion.1), slice={[0:63:2], [1:48:2], [0:24:1]} | slice | bytes 73728 | tf_op jit(solution)/shard_map/slice | solution.py:49
  167.3 3.7 %slice.148 = bf16[32,24,24]{0,2,1:T(8,128)(2,1)S(1)} slice(bf16[65,49,24]{0,2,1:T(8,128)(2,1)S(1)} %maximum_maximum_fusion.1), slice={[0:63:2], [0:47:2], [0:24:1]} | slice | bytes 73728 | tf_op jit(solution)/shard_map/slice | solution.py:49
  172.9 1.1 fusion.58
  174.0 1.0 convolution_add_fusion.4
  175.0 1.0 convolution_add_fusion.3
  176.0 1.0 fusion.23
  177.0 1.0 fusion.24
  184.0 2.1 collective-permute-start.3
  188.1 1.0 maximum_maximum_fusion
  193.6 81.5 %all_to_all.33 = bf16[32,16,12,512]{3,1,2,0:T(8,128)(2,1)S(1)} all-to-all(bf16[32,16,12,512]{3,1,2,0:T(8,128)(2,1)S(1)} %stack.2), channel_id=1, replica_groups=mesh['lat'=4,'lon'=32] {'lon'}, dimensions={0} | all-to-all | bytes 12582912 | tf_op jit(solution)/shard_map/all_to_all | solution.py:129
  275.1 6.4 %copy.41 = bf16[16,384,512]{2,1,0:T(8,128)(2,1)} copy(bf16[16,384,512]{2,0,1:T(8,128)(2,1)S(1)} %bitcast.131) | data formatting | bytes 12582912 | tf_op jit(solution)/shard_map/reshape | solution.py:128
  (223 shorter events, 40.2 us)
Async XLA Ops:
  1.4 21.0 %all-to-all-start = ((s32[1,128,4]{2,0,1:T(1,128)}), s32[1,128,4]{2,0,1:T(1,128)S(1)}, u32[]{:S(2)}, u32[]{:S(2)}) async-start(s32[1,128,4]{2,0,1:T(1,128)} %copy.28), calls=%async_computation | async-start | bytes 131072 | tf_op jit(solution)/shard_map/all_to_all | solution.py:79
  13.7 57.5 %copy-start.10 = (bf16[6,23]{1,0:T(8,128)(2,1)S(1)}, bf16[6,23]{1,0:T(8,128)(2,1)}, u32[]{:S(2)}) copy-start(bf16[6,23]{1,0:T(8,128)(2,1)} %param.13) | copy-start | bytes 832
  36.3 34.9 %all-to-all-start.1 = ((bf16[1,128,4,8,256]{4,3,2,0,1:T(8,128)(2,1)}), bf16[1,128,4,8,256]{4,3,2,0,1:T(8,128)(2,1)S(1)}, u32[]{:S(2)}, u32[]{:S(2)}) async-start(bf16[1,128,4,8,256]{4,3,2,0,1:T(8,128)(2,1)} %bitcast.140), calls=%async_computation.1 | async-start | bytes 4194304 | tf_op jit(solution)/shard_map/all_to_all | solution.py:78
  139.7 6.2 %collective-permute-start = (bf16[64,1,24]{2,1,0:T(2,128)(2,1)S(1)}, bf16[64,1,24]{2,1,0:T(2,128)(2,1)S(1)}, u32[]{:S(2)}, u32[]{:S(2)}) collective-permute-start(bf16[64,1,24]{2,1,0:T(2,128)(2,1)S(1)} %slice.192), channel_id=1, source_target_pairs={{0,1},{1,2},{2,3},{3,4},{4,5},{5,6},{6,7},{7,8},{8,9},{9,10},{10,1... | collective-permute-start | bytes 9224 | tf_op jit(solution)/shard_map/ppermute | solution.py:14
  146.8 11.5 %collective-permute-start.1 = (bf16[1,49,24]{0,2,1:T(8,128)(2,1)}, bf16[1,49,24]{0,2,1:T(8,128)(2,1)}, u32[]{:S(2)}, u32[]{:S(2)}) collective-permute-start(bf16[1,49,24]{0,2,1:T(8,128)(2,1)} %fusion.25), channel_id=1, source_target_pairs={{0,32},{32,64},{64,96},{1,33},{33,65},{65,97},{2,34},{34,66},{66,9... | collective-permute-start | bytes 7064 | tf_op jit(solution)/shard_map/ppermute | solution.py:20
  172.5 3.5 %copy-start = (f32[768,256]{1,0:T(8,128)S(1)}, f32[768,256]{1,0:T(8,128)}, u32[]{:S(2)}) copy-start(f32[768,256]{1,0:T(8,128)} %fusion.51) | copy-start | bytes 2359300
  172.6 3.4 %copy-start.9 = (bf16[768,24]{0,1:T(8,128)(2,1)S(1)}, bf16[768,24]{0,1:T(8,128)(2,1)}, u32[]{:S(2)}) copy-start(bf16[768,24]{0,1:T(8,128)(2,1)} %reshape.163) | copy-start | bytes 110596
  175.0 2.1 copy-start.8
  177.0 1.0 copy-start.12
  178.3 5.1 %collective-permute-start.2 = (bf16[32,1,256]{2,1,0:T(2,128)(2,1)S(1)}, bf16[32,1,256]{2,1,0:T(2,128)(2,1)S(1)}, u32[]{:S(2)}, u32[]{:S(2)}) collective-permute-start(bf16[32,1,256]{2,1,0:T(2,128)(2,1)S(1)} %slice.195), channel_id=1, source_target_pairs={{0,1},{1,2},{2,3},{3,4},{4,5},{5,6},{6,7},{7,8},{8,9},{9,10},{10,1... | collective-permute-start | bytes 49160 | tf_op jit(solution)/shard_map/ppermute | solution.py:14
  183.4 7.1 %copy-start.1 = (bf16[9,256,512]{2,1,0:T(8,128)(2,1)S(1)}, bf16[9,256,512]{2,1,0:T(8,128)(2,1)}, u32[]{:S(2)}) copy-start(bf16[9,256,512]{2,1,0:T(8,128)(2,1)} %param.16) | copy-start | bytes 7077892
  183.4 2.7 copy-start.7
  184.0 4.1 %collective-permute-start.3 = (bf16[1,25,256]{2,1,0:T(8,128)(2,1)}, bf16[1,25,256]{2,1,0:T(8,128)(2,1)S(1)}, u32[]{:S(2)}, u32[]{:S(2)}) collective-permute-start(bf16[1,25,256]{2,1,0:T(8,128)(2,1)} %fusion.45), channel_id=1, source_target_pairs={{0,32},{32,64},{64,96},{1,33},{33,65},{65,97},{2,34},{34,66},{66,9... | collective-permute-start | bytes 38408 | tf_op jit(solution)/shard_map/ppermute | solution.py:20
  189.1 2.0 copy-start.6
  190.4 1.0 copy-start.5
  190.7 0.9 copy-start.4
  191.2 0.9 copy-start.3
  191.4 0.9 copy-start.2
  191.8 0.7 copy-start.11
